TPU v7x, 256 devices: a whole 4x4x8 slice. The times are simulated.
256 devices in a mesh: row: 16 (over z, core), col: 16 (over x, y).
Axes of the slice: x: 4, y: 4, z: 8, core: 2. Of those that a mesh axis runs over, the one named last changes fastest.
Arguments:
- kernel: float32 [12288, 12288], P('row', 'col'), may hold values from 0 to 3.1, as said below
Outputs:
- factored: float32 [12288, 12288], P('row', 'col')
Inputs may be any that keep to these rules, and one draw needn't show every extreme that they name: kernel is the block-cyclic storage of a symmetric positive definite matrix whose least eigenvalue is 0.5 or more.
All inputs are finite; a program needn't handle non-finite values.
Results may differ from a plain program's by a relative error of at most 0.0003.
Values sent between devices are 32-bit elements; how exact they have to be, the bound alone decides.
A program may use at most 64 MiB of HBM per device.

v0:
```python
import jax
import jax.numpy as jnp
from jax import lax
from jax.sharding import PartitionSpec as P

NB = 256
SUBPANELS = 4


def broadcast(value, axis, source):
    kept = jnp.where(lax.axis_index(axis) == source, value, 0).astype(value.dtype)
    return lax.psum(kept, axis)


def lower_inverse(factor):
    ident = jnp.eye(factor.shape[0], dtype=jnp.float32)
    return jax.scipy.linalg.solve_triangular(factor, ident, lower=True)


def outer_product(left, right):
    return lax.dot_general(
        left,
        right,
        (((1,), (1,)), ((), ())),
        precision=lax.Precision.HIGHEST,
        preferred_element_type=jnp.float32,
    )


def body(kernel):
    width_sub = NB
    rows_total, cols_total = kernel.shape
    rows_blocks = rows_total // width_sub
    cols_blocks = cols_total // width_sub
    row_count = lax.axis_size("row")
    col_count = lax.axis_size("col")
    row_index = lax.axis_index("row")
    col_index = lax.axis_index("col")
    row_global = jnp.arange(rows_total, dtype=jnp.int32) // width_sub * row_count + row_index
    col_global = jnp.arange(cols_total, dtype=jnp.int32) // width_sub * col_count + col_index
    identity = jnp.eye(width_sub, dtype=jnp.float32)
    matrix = kernel
    for sub_step in range(SUBPANELS):
        factor_matrix = matrix
        owner_row = sub_step % row_count
        local_row = sub_step // row_count
        owner_col = sub_step % col_count
        local_col = sub_step // col_count
        column_slab = factor_matrix[:, local_col * width_sub : (local_col + 1) * width_sub]
        corner = column_slab[local_row * width_sub : (local_row + 1) * width_sub]
        diag = broadcast(corner, "row", owner_row)
        diag = jnp.where(col_index == owner_col, diag, identity)
        factor_factor = jnp.linalg.cholesky(diag)
        factor_solved = outer_product(column_slab, lower_inverse(factor_factor))
        stacked = jnp.tile(factor_factor, (rows_blocks, 1))
        position = row_global[:, None]
        panel = broadcast(
            jnp.where(
                position > sub_step, factor_solved, jnp.where(position == sub_step, stacked, 0.0)
            ),
            "col",
            owner_col,
        )
        pieces = []
        for local_blk in range(cols_blocks):
            global_blk = local_blk * col_count + col_index
            piece = lax.dynamic_slice_in_dim(
                panel, global_blk // row_count * width_sub, width_sub, 0
            )
            pieces.append(broadcast(piece, "row", global_blk % row_count))
        across = jnp.concatenate(pieces, axis=0)
        kept = jnp.where(col_index == owner_col, panel, column_slab)
        factor_matrix = factor_matrix.at[
            :, local_col * width_sub : (local_col + 1) * width_sub
        ].set(kept)
        matrix, panel, across = (factor_matrix, panel, across)
        region = (row_global[:, None] > sub_step) & (col_global[None, :] > sub_step)
        matrix = matrix - jnp.where(region, outer_product(panel, across), 0.0)
    corner_zero = (row_global[:, None] < SUBPANELS) & (col_global[None, :] >= SUBPANELS)
    return jnp.where(corner_zero, 0.0, matrix)


def solution(mesh):
    return jax.shard_map(
        body, mesh=mesh, in_specs=(P("row", "col"),), out_specs=P("row", "col"), check_vma=False
    )
```

profile of v0, /device:TPU:1, one launch (start us, length us, event | category | flops | bytes accessed | tf_op | source)
XLA Modules:
  0.0 1590.1 jit_solution(16395808268641596586)
XLA Ops:
  9.4 112.4 %all-reduce.18.cloned.1.call-done = f32[256,256]{0,1:T(8,128)} async-done(((f32[256,256]{0,1:T(8,128)}), f32[256,256]{0,1:T(8,128)}) %all-reduce.18.cloned.1.call-update) | async-done | bytes 262160 | tf_op jit(solution)/shard_map/psum | solution.py:12
  124.0 11.7 cholesky.214
  146.1 11.7 cholesky.231
  164.5 19.7 %custom-call.18 = f32[2,128,128]{1,2,0:T(8,128)S(1)} custom-call(f32[2,128,128]{2,1,0:T(8,128)S(1)} %get-tuple-element.81), custom_call_target="InvertDiagBlocksLowerTriangular" | custom-call | tf_op jit(solution)/shard_map/jit(_solve_triangular)/triangular_solve | solution.py:17
  191.7 92.6 %all-reduce.20.cloned.1.call-done = f32[768,256]{0,1:T(8,128)} async-done(((f32[768,256]{0,1:T(8,128)}), f32[768,256]{0,1:T(8,128)}) %all-reduce.20.cloned.1.call-update) | async-done | bytes 786448 | tf_op jit(solution)/shard_map/psum | solution.py:12
  287.3 111.3 %all-reduce.40.cloned.1.call-done = (f32[256,256]{0,1:T(8,128)}, f32[256,256]{0,1:T(8,128)}, f32[256,256]{0,1:T(8,128)}) async-done(((f32[256,256]{0,1:T(8,128)}, f32[256,256]{0,1:T(8,128)}, f32[256,256]{0,1:T(8,128)}), (f32[256,256]{0,1:T(8,128)}, f32[256,256]{0,1:T(8,128)}, f32[256,256]{0,1:T(8,128)})) %all-reduce.40.cloned.1.call-update) | async-done | bytes 786448 | tf_op jit(solution)/shard_map/psum | solution.py:12
  404.6 108.8 %all-reduce.22.cloned.1.call-done = f32[256,256]{0,1:T(8,128)} async-done(((f32[256,256]{0,1:T(8,128)}), f32[256,256]{0,1:T(8,128)}) %all-reduce.22.cloned.1.call-update) | async-done | bytes 262160 | tf_op jit(solution)/shard_map/psum | solution.py:12
  513.7 11.7 cholesky.248
  535.7 11.7 cholesky.265
  555.2 19.7 %custom-call.20 = f32[2,128,128]{1,2,0:T(8,128)S(1)} custom-call(f32[2,128,128]{2,1,0:T(8,128)S(1)} %get-tuple-element.82), custom_call_target="InvertDiagBlocksLowerTriangular" | custom-call | tf_op jit(solution)/shard_map/jit(_solve_triangular)/triangular_solve | solution.py:17
  581.8 95.2 %all-reduce.24.cloned.1.call-done = f32[768,256]{0,1:T(8,128)} async-done(((f32[768,256]{0,1:T(8,128)}), f32[768,256]{0,1:T(8,128)}) %all-reduce.24.cloned.1.call-update) | async-done | bytes 786448 | tf_op jit(solution)/shard_map/psum | solution.py:12
  680.0 111.2 %all-reduce.38.cloned.1.call-done = (f32[256,256]{0,1:T(8,128)}, f32[256,256]{0,1:T(8,128)}, f32[256,256]{0,1:T(8,128)}) async-done(((f32[256,256]{0,1:T(8,128)}, f32[256,256]{0,1:T(8,128)}, f32[256,256]{0,1:T(8,128)}), (f32[256,256]{0,1:T(8,128)}, f32[256,256]{0,1:T(8,128)}, f32[256,256]{0,1:T(8,128)})) %all-reduce.38.cloned.1.call-update) | async-done | bytes 786448 | tf_op jit(solution)/shard_map/psum | solution.py:12
  796.5 108.9 %all-reduce.26.cloned.1.call-done = f32[256,256]{0,1:T(8,128)} async-done(((f32[256,256]{0,1:T(8,128)}), f32[256,256]{0,1:T(8,128)}) %all-reduce.26.cloned.1.call-update) | async-done | bytes 262160 | tf_op jit(solution)/shard_map/psum | solution.py:12
  905.6 11.7 cholesky.282
  927.6 11.7 cholesky.299
  946.7 19.7 %custom-call.22 = f32[2,128,128]{1,2,0:T(8,128)S(1)} custom-call(f32[2,128,128]{2,1,0:T(8,128)S(1)} %get-tuple-element.83), custom_call_target="InvertDiagBlocksLowerTriangular" | custom-call | tf_op jit(solution)/shard_map/jit(_solve_triangular)/triangular_solve | solution.py:17
  973.3 95.2 %all-reduce.28.cloned.1.call-done = f32[768,256]{0,1:T(8,128)} async-done(((f32[768,256]{0,1:T(8,128)}), f32[768,256]{0,1:T(8,128)}) %all-reduce.28.cloned.1.call-update) | async-done | bytes 786448 | tf_op jit(solution)/shard_map/psum | solution.py:12
  1071.5 111.3 %all-reduce.36.cloned.1.call-done = (f32[256,256]{0,1:T(8,128)}, f32[256,256]{0,1:T(8,128)}, f32[256,256]{0,1:T(8,128)}) async-done(((f32[256,256]{0,1:T(8,128)}, f32[256,256]{0,1:T(8,128)}, f32[256,256]{0,1:T(8,128)}), (f32[256,256]{0,1:T(8,128)}, f32[256,256]{0,1:T(8,128)}, f32[256,256]{0,1:T(8,128)})) %all-reduce.36.cloned.1.call-update) | async-done | bytes 786448 | tf_op jit(solution)/shard_map/psum | solution.py:12
  1188.8 108.8 %all-reduce.30.cloned.1.call-done = f32[256,256]{0,1:T(8,128)} async-done(((f32[256,256]{0,1:T(8,128)}), f32[256,256]{0,1:T(8,128)}) %all-reduce.30.cloned.1.call-update) | async-done | bytes 262160 | tf_op jit(solution)/shard_map/psum | solution.py:12
  1297.8 11.7 cholesky.316
  1319.9 11.7 cholesky.333
  1339.3 19.7 %custom-call.24 = f32[2,128,128]{1,2,0:T(8,128)S(1)} custom-call(f32[2,128,128]{2,1,0:T(8,128)S(1)} %get-tuple-element.84), custom_call_target="InvertDiagBlocksLowerTriangular" | custom-call | tf_op jit(solution)/shard_map/jit(_solve_triangular)/triangular_solve | solution.py:17
  1365.2 95.2 %all-reduce.32.cloned.1.call-done = f32[768,256]{0,1:T(8,128)} async-done(((f32[768,256]{0,1:T(8,128)}), f32[768,256]{0,1:T(8,128)}) %all-reduce.32.cloned.1.call-update) | async-done | bytes 786448 | tf_op jit(solution)/shard_map/psum | solution.py:12
  1463.3 111.3 %all-reduce.34.cloned.1.call-done = (f32[256,256]{0,1:T(8,128)}, f32[256,256]{0,1:T(8,128)}, f32[256,256]{0,1:T(8,128)}) async-done(((f32[256,256]{0,1:T(8,128)}, f32[256,256]{0,1:T(8,128)}, f32[256,256]{0,1:T(8,128)}), (f32[256,256]{0,1:T(8,128)}, f32[256,256]{0,1:T(8,128)}, f32[256,256]{0,1:T(8,128)})) %all-reduce.34.cloned.1.call-update) | async-done | bytes 786448 | tf_op jit(solution)/shard_map/psum | solution.py:12
  (180 shorter events, 151.4 us)
Async XLA Ops:
  6.5 115.3 %all-reduce.18.cloned.1.call-start = ((), (), s32[]{:S(2)}) async-start(), calls=%async_computation | async-start | bytes 524288 | tf_op jit(solution)/shard_map/psum | solution.py:12
  9.3 275.0 %all-reduce.20.cloned.1.call-start = ((), (), s32[]{:S(2)}) async-start(), calls=%async_computation.1 | async-start | bytes 1572864 | tf_op jit(solution)/shard_map/psum | solution.py:12
  191.0 207.6 %all-reduce.40.cloned.1.call-start = ((), (), s32[]{:S(2)}) async-start(), calls=%async_computation.11 | async-start | bytes 1572864 | tf_op jit(solution)/shard_map/psum | solution.py:12
  284.3 2.2 copy-start.5
  286.4 227.0 %all-reduce.22.cloned.1.call-start = ((), (), s32[]{:S(2)}) async-start(), calls=%async_computation.2 | async-start | bytes 524288 | tf_op jit(solution)/shard_map/psum | solution.py:12
  402.2 1.4 copy-start
  404.3 272.6 %all-reduce.24.cloned.1.call-start = ((), (), s32[]{:S(2)}) async-start(), calls=%async_computation.3 | async-start | bytes 1572864 | tf_op jit(solution)/shard_map/psum | solution.py:12
  550.8 27.9 %copy-start.1 = (f32[768,768]{0,1:T(8,128)S(1)}, f32[768,768]{0,1:T(8,128)}, u32[]{:S(2)}) copy-start(f32[768,768]{0,1:T(8,128)} %copy-done) | copy-start | bytes 7077892
  581.7 209.6 %all-reduce.38.cloned.1.call-start = ((), (), s32[]{:S(2)}) async-start(), calls=%async_computation.10 | async-start | bytes 1572864 | tf_op jit(solution)/shard_map/psum | solution.py:12
  676.9 2.2 copy-start.7
  679.1 226.2 %all-reduce.26.cloned.1.call-start = ((), (), s32[]{:S(2)}) async-start(), calls=%async_computation.4 | async-start | bytes 524288 | tf_op jit(solution)/shard_map/psum | solution.py:12
  680.0 111.3 %copy-start.2 = (f32[768,768]{0,1:T(8,128)}, f32[768,768]{0,1:T(8,128)S(1)}, u32[]{:S(2)}) copy-start(f32[768,768]{0,1:T(8,128)S(1)} %fusion.6) | copy-start | bytes 7077892
  796.2 272.3 %all-reduce.28.cloned.1.call-start = ((), (), s32[]{:S(2)}) async-start(), calls=%async_computation.5 | async-start | bytes 1572864 | tf_op jit(solution)/shard_map/psum | solution.py:12
  973.2 209.5 %all-reduce.36.cloned.1.call-start = ((), (), s32[]{:S(2)}) async-start(), calls=%async_computation.9 | async-start | bytes 1572864 | tf_op jit(solution)/shard_map/psum | solution.py:12
  1068.5 2.2 copy-start.8
  1070.6 227.0 %all-reduce.30.cloned.1.call-start = ((), (), s32[]{:S(2)}) async-start(), calls=%async_computation.6 | async-start | bytes 524288 | tf_op jit(solution)/shard_map/psum | solution.py:12
  1186.3 1.4 copy-start.3
  1188.5 271.9 %all-reduce.32.cloned.1.call-start = ((), (), s32[]{:S(2)}) async-start(), calls=%async_computation.7 | async-start | bytes 1572864 | tf_op jit(solution)/shard_map/psum | solution.py:12
  1335.0 27.3 %copy-start.4 = (f32[768,768]{0,1:T(8,128)S(1)}, f32[768,768]{0,1:T(8,128)}, u32[]{:S(2)}) copy-start(f32[768,768]{0,1:T(8,128)} %copy-done.3) | copy-start | bytes 7077892
  1365.1 209.5 %all-reduce.34.cloned.1.call-start = ((), (), s32[]{:S(2)}) async-start(), calls=%async_computation.8 | async-start | bytes 1572864 | tf_op jit(solution)/shard_map/psum | solution.py:12
  1460.4 2.1 copy-start.6
Sparse Core Ops, SparseCore 0:
  9.7 112.1 all-reduce.17
  191.1 93.1 all-reduce.19
  286.9 111.6 all-reduce.39
  404.4 108.9 all-reduce.21
  581.8 95.0 all-reduce.23
  679.5 111.7 all-reduce.37
  796.3 108.9 all-reduce.25
  973.4 95.0 all-reduce.27
  1071.0 111.6 all-reduce.35
  1188.6 108.9 all-reduce.29
  1365.3 95.0 all-reduce.31
  1462.9 111.6 all-reduce.33
where the time goes:
time: 1600 us; the launch traced here: 1590 us
  waiting for transfers between devices  1260 us (79%)
  other arithmetic  237 us (15%)
  matrix products  36 us (2%)
  local copies, waits for them, and re-layouts  32.7 us (2%)
  between operations  19.7 us (1%)
    psum x12, waiting for transfers between devices, broadcast(): return lax.psum(kept, axis)  1260 us
    another operation x27, other arithmetic, body(): factor_factor = jnp.linalg.cholesky(diag)  138 us
    another operation x9, other arithmetic, lower_inverse(): return jax.scipy.linalg.solve_triangular(factor, ident, lower=True)  81.6 us
  transfers between devices with their start and end apart: 12, of which 12 were waited for; matrix products, arithmetic and copies ran while one was open for 0% of the time, Pallas kernels for 0%

commit v1 on v0

--- a/solution.py
+++ b/solution.py
@@ -9,7 +9,7 @@
 
 def broadcast(value, axis, source):
     kept = jnp.where(lax.axis_index(axis) == source, value, 0).astype(value.dtype)
-    return lax.psum(kept, axis)
+    return jnp.sum(lax.all_gather(kept, axis), axis=0)
 
 
 def lower_inverse(factor):

time: 1600 us -> 1500 us (0.938)
  waiting for transfers between devices: 1260 us -> 993 us
  local copies, waits for them, and re-layouts: 32.7 us -> 161 us
  other arithmetic: 237 us -> 281 us
    psum x12 -> x0, waiting for transfers between devices: 1260 us -> none  [broadcast(): return lax.psum(kept, axis)]
    all_gather x0 -> x20, waiting for transfers between devices: none -> 988 us  [broadcast(): return jnp.sum(lax.all_gather(kept, axis), axis=0)]
    unnamed x19 -> x63, local copies, waits for them, and re-layouts: 4.86 us -> 134 us
    reduce_sum x0 -> x20, other arithmetic: none -> 49.8 us  [broadcast(): return jnp.sum(lax.all_gather(kept, axis), axis=0)]
  transfers between devices with their start and end apart: 12 -> 20, of which waited for: 12 -> 20; matrix products, arithmetic and copies ran while one was open for 0% -> 4% of each run, Pallas kernels for 0% -> 0%
where the time goes in v1:
time: 1500 us; the launch traced here: 1490 us
  waiting for transfers between devices  993 us (66%)
  other arithmetic  281 us (19%)
  local copies, waits for them, and re-layouts  161 us (11%)
  matrix products  38 us (3%)
  between operations  19.8 us (1%)
    all_gather x20, waiting for transfers between devices, broadcast(): return jnp.sum(lax.all_gather(kept, axis), axis=0)  988 us
    another operation x27, other arithmetic, body(): factor_factor = jnp.linalg.cholesky(diag)  138 us
    unnamed x63, local copies, waits for them, and re-layouts  134 us
    another operation x9, other arithmetic, lower_inverse(): return jax.scipy.linalg.solve_triangular(factor, ident, lower=True)  82.8 us
    reduce_sum x20, other arithmetic, broadcast(): return jnp.sum(lax.all_gather(kept, axis), axis=0)  49.8 us
  transfers between devices with their start and end apart: 20, of which 20 were waited for; matrix products, arithmetic and copies ran while one was open for 4% of the time, Pallas kernels for 0%

profile of v1, /device:TPU:1, one launch (start us, length us, event | category | flops | bytes accessed | tf_op | source)
XLA Modules:
  0.0 1494.8 jit_solution(12712934042234864595)
XLA Ops:
  9.4 46.4 %all-gather.41.cloned.1.call-done = f32[4096,256]{0,1:T(8,128)} async-done(((f32[256,256]{0,1:T(8,128)}), f32[4096,256]{0,1:T(8,128)}) %all-gather.41.cloned.1.call-update) | async-done | bytes 4194320 | tf_op jit(solution)/shard_map/all_gather | solution.py:12
  103.3 20.1 %custom-call.18 = f32[2,128,128]{1,2,0:T(8,128)S(1)} custom-call(f32[2,128,128]{2,1,0:T(8,128)S(1)} %get-tuple-element.81), custom_call_target="InvertDiagBlocksLowerTriangular" | custom-call | tf_op jit(solution)/shard_map/jit(_solve_triangular)/triangular_solve | solution.py:17
  130.3 93.2 %all-gather.43.cloned.1.call-done = f32[12288,256]{0,1:T(8,128)} async-done(((f32[768,256]{0,1:T(8,128)}), f32[12288,256]{0,1:T(8,128)}) %all-gather.43.cloned.1.call-update) | async-done | bytes 12582928 | tf_op jit(solution)/shard_map/all_gather | solution.py:12
  248.3 39.5 %all-gather.49.cloned.1.call-done = f32[4096,256]{0,1:T(8,128)} async-done(((f32[256,256]{0,1:T(8,128)}), f32[4096,256]{0,1:T(8,128)}) %all-gather.49.cloned.1.call-update) | async-done | bytes 4194320 | tf_op jit(solution)/shard_map/all_gather | solution.py:12
  293.7 36.6 %all-gather.47.cloned.1.call-done = f32[4096,256]{0,1:T(8,128)} async-done(((f32[256,256]{0,1:T(8,128)}), f32[4096,256]{0,1:T(8,128)}) %all-gather.47.cloned.1.call-update) | async-done | bytes 4194320 | tf_op jit(solution)/shard_map/all_gather | solution.py:12
  337.9 34.9 %all-gather.45.cloned.1.call-done = f32[4096,256]{0,1:T(8,128)} async-done(((f32[256,256]{0,1:T(8,128)}), f32[4096,256]{0,1:T(8,128)}) %all-gather.45.cloned.1.call-update) | async-done | bytes 4194320 | tf_op jit(solution)/shard_map/all_gather | solution.py:12
  382.5 40.8 %all-gather.51.cloned.1.call-done = f32[4096,256]{0,1:T(8,128)} async-done(((f32[256,256]{0,1:T(8,128)}), f32[4096,256]{0,1:T(8,128)}) %all-gather.51.cloned.1.call-update) | async-done | bytes 4194320 | tf_op jit(solution)/shard_map/all_gather | solution.py:12
  471.4 19.9 %custom-call.20 = f32[2,128,128]{1,2,0:T(8,128)S(1)} custom-call(f32[2,128,128]{2,1,0:T(8,128)S(1)} %get-tuple-element.82), custom_call_target="InvertDiagBlocksLowerTriangular" | custom-call | tf_op jit(solution)/shard_map/jit(_solve_triangular)/triangular_solve | solution.py:17
  498.2 93.3 %all-gather.53.cloned.1.call-done = f32[12288,256]{0,1:T(8,128)} async-done(((f32[768,256]{0,1:T(8,128)}), f32[12288,256]{0,1:T(8,128)}) %all-gather.53.cloned.1.call-update) | async-done | bytes 12582928 | tf_op jit(solution)/shard_map/all_gather | solution.py:12
  616.1 39.8 %all-gather.59.cloned.1.call-done = f32[4096,256]{0,1:T(8,128)} async-done(((f32[256,256]{0,1:T(8,128)}), f32[4096,256]{0,1:T(8,128)}) %all-gather.59.cloned.1.call-update) | async-done | bytes 4194320 | tf_op jit(solution)/shard_map/all_gather | solution.py:12
  661.8 36.7 %all-gather.57.cloned.1.call-done = f32[4096,256]{0,1:T(8,128)} async-done(((f32[256,256]{0,1:T(8,128)}), f32[4096,256]{0,1:T(8,128)}) %all-gather.57.cloned.1.call-update) | async-done | bytes 4194320 | tf_op jit(solution)/shard_map/all_gather | solution.py:12
  706.1 34.9 %all-gather.55.cloned.1.call-done = f32[4096,256]{0,1:T(8,128)} async-done(((f32[256,256]{0,1:T(8,128)}), f32[4096,256]{0,1:T(8,128)}) %all-gather.55.cloned.1.call-update) | async-done | bytes 4194320 | tf_op jit(solution)/shard_map/all_gather | solution.py:12
  749.9 40.8 %all-gather.61.cloned.1.call-done = f32[4096,256]{0,1:T(8,128)} async-done(((f32[256,256]{0,1:T(8,128)}), f32[4096,256]{0,1:T(8,128)}) %all-gather.61.cloned.1.call-update) | async-done | bytes 4194320 | tf_op jit(solution)/shard_map/all_gather | solution.py:12
  838.7 20.1 %custom-call.22 = f32[2,128,128]{1,2,0:T(8,128)S(1)} custom-call(f32[2,128,128]{2,1,0:T(8,128)S(1)} %get-tuple-element.83), custom_call_target="InvertDiagBlocksLowerTriangular" | custom-call | tf_op jit(solution)/shard_map/jit(_solve_triangular)/triangular_solve | solution.py:17
  865.7 93.3 %all-gather.63.cloned.1.call-done = f32[12288,256]{0,1:T(8,128)} async-done(((f32[768,256]{0,1:T(8,128)}), f32[12288,256]{0,1:T(8,128)}) %all-gather.63.cloned.1.call-update) | async-done | bytes 12582928 | tf_op jit(solution)/shard_map/all_gather | solution.py:12
  983.2 40.2 %all-gather.65.cloned.1.call-done = f32[4096,256]{0,1:T(8,128)} async-done(((f32[256,256]{0,1:T(8,128)}), f32[4096,256]{0,1:T(8,128)}) %all-gather.65.cloned.1.call-update) | async-done | bytes 4194320 | tf_op jit(solution)/shard_map/all_gather | solution.py:12
  1029.2 36.6 %all-gather.69.cloned.1.call-done = f32[4096,256]{0,1:T(8,128)} async-done(((f32[256,256]{0,1:T(8,128)}), f32[4096,256]{0,1:T(8,128)}) %all-gather.69.cloned.1.call-update) | async-done | bytes 4194320 | tf_op jit(solution)/shard_map/all_gather | solution.py:12
  1073.3 34.9 %all-gather.67.cloned.1.call-done = f32[4096,256]{0,1:T(8,128)} async-done(((f32[256,256]{0,1:T(8,128)}), f32[4096,256]{0,1:T(8,128)}) %all-gather.67.cloned.1.call-update) | async-done | bytes 4194320 | tf_op jit(solution)/shard_map/all_gather | solution.py:12
  1118.0 40.8 %all-gather.71.cloned.1.call-done = f32[4096,256]{0,1:T(8,128)} async-done(((f32[256,256]{0,1:T(8,128)}), f32[4096,256]{0,1:T(8,128)}) %all-gather.71.cloned.1.call-update) | async-done | bytes 4194320 | tf_op jit(solution)/shard_map/all_gather | solution.py:12
  1206.9 19.8 %custom-call.24 = f32[2,128,128]{1,2,0:T(8,128)S(1)} custom-call(f32[2,128,128]{2,1,0:T(8,128)S(1)} %get-tuple-element.84), custom_call_target="InvertDiagBlocksLowerTriangular" | custom-call | tf_op jit(solution)/shard_map/jit(_solve_triangular)/triangular_solve | solution.py:17
  1233.0 93.3 %all-gather.73.cloned.1.call-done = f32[12288,256]{0,1:T(8,128)} async-done(((f32[768,256]{0,1:T(8,128)}), f32[12288,256]{0,1:T(8,128)}) %all-gather.73.cloned.1.call-update) | async-done | bytes 12582928 | tf_op jit(solution)/shard_map/all_gather | solution.py:12
  1350.4 40.2 %all-gather.79.cloned.1.call-done = f32[4096,256]{0,1:T(8,128)} async-done(((f32[256,256]{0,1:T(8,128)}), f32[4096,256]{0,1:T(8,128)}) %all-gather.79.cloned.1.call-update) | async-done | bytes 4194320 | tf_op jit(solution)/shard_map/all_gather | solution.py:12
  1396.5 36.7 %all-gather.77.cloned.1.call-done = f32[4096,256]{0,1:T(8,128)} async-done(((f32[256,256]{0,1:T(8,128)}), f32[4096,256]{0,1:T(8,128)}) %all-gather.77.cloned.1.call-update) | async-done | bytes 4194320 | tf_op jit(solution)/shard_map/all_gather | solution.py:12
  1440.0 35.6 %all-gather.75.cloned.1.call-done = f32[4096,256]{0,1:T(8,128)} async-done(((f32[256,256]{0,1:T(8,128)}), f32[4096,256]{0,1:T(8,128)}) %all-gather.75.cloned.1.call-update) | async-done | bytes 4194320 | tf_op jit(solution)/shard_map/all_gather | solution.py:12
  (268 shorter events, 421.6 us)
Async XLA Ops:
  6.5 49.3 %all-gather.41.cloned.1.call-start = ((), (), s32[]{:S(2)}) async-start(), calls=%async_computation | async-start | bytes 4456448 | tf_op jit(solution)/shard_map/all_gather | solution.py:12
  9.3 214.2 %all-gather.43.cloned.1.call-start = ((), (), s32[]{:S(2)}) async-start(), calls=%async_computation.1 | async-start | bytes 13369344 | tf_op jit(solution)/shard_map/all_gather | solution.py:12
  61.2 11.8 copy-start.17
  130.1 157.7 %all-gather.49.cloned.1.call-start = ((), (), s32[]{:S(2)}) async-start(), calls=%async_computation.4 | async-start | bytes 4456448 | tf_op jit(solution)/shard_map/all_gather | solution.py:12
  245.4 84.9 %all-gather.47.cloned.1.call-start = ((), (), s32[]{:S(2)}) async-start(), calls=%async_computation.3 | async-start | bytes 4456448 | tf_op jit(solution)/shard_map/all_gather | solution.py:12
  246.0 126.7 %all-gather.45.cloned.1.call-start = ((), (), s32[]{:S(2)}) async-start(), calls=%async_computation.2 | async-start | bytes 4456448 | tf_op jit(solution)/shard_map/all_gather | solution.py:12
  246.6 176.7 %all-gather.51.cloned.1.call-start = ((), (), s32[]{:S(2)}) async-start(), calls=%async_computation.5 | async-start | bytes 4456448 | tf_op jit(solution)/shard_map/all_gather | solution.py:12
  382.5 209.0 %all-gather.53.cloned.1.call-start = ((), (), s32[]{:S(2)}) async-start(), calls=%async_computation.6 | async-start | bytes 13369344 | tf_op jit(solution)/shard_map/all_gather | solution.py:12
  428.7 66.5 %copy-start.1 = (f32[768,768]{0,1:T(8,128)S(1)}, f32[768,768]{0,1:T(8,128)}, u32[]{:S(2)}) copy-start(f32[768,768]{0,1:T(8,128)} %copy-done) | copy-start | bytes 7077892
  498.1 157.8 %all-gather.59.cloned.1.call-start = ((), (), s32[]{:S(2)}) async-start(), calls=%async_computation.9 | async-start | bytes 4456448 | tf_op jit(solution)/shard_map/all_gather | solution.py:12
  613.5 85.0 %all-gather.57.cloned.1.call-start = ((), (), s32[]{:S(2)}) async-start(), calls=%async_computation.8 | async-start | bytes 4456448 | tf_op jit(solution)/shard_map/all_gather | solution.py:12
  614.2 126.7 %all-gather.55.cloned.1.call-start = ((), (), s32[]{:S(2)}) async-start(), calls=%async_computation.7 | async-start | bytes 4456448 | tf_op jit(solution)/shard_map/all_gather | solution.py:12
  614.8 175.9 %all-gather.61.cloned.1.call-start = ((), (), s32[]{:S(2)}) async-start(), calls=%async_computation.10 | async-start | bytes 4456448 | tf_op jit(solution)/shard_map/all_gather | solution.py:12
  616.1 90.0 %copy-start.2 = (f32[768,768]{0,1:T(8,128)}, f32[768,768]{0,1:T(8,128)S(1)}, u32[]{:S(2)}) copy-start(f32[768,768]{0,1:T(8,128)S(1)} %fusion.6) | copy-start | bytes 7077892
  749.9 209.1 %all-gather.63.cloned.1.call-start = ((), (), s32[]{:S(2)}) async-start(), calls=%async_computation.11 | async-start | bytes 13369344 | tf_op jit(solution)/shard_map/all_gather | solution.py:12
  865.6 157.7 %all-gather.65.cloned.1.call-start = ((), (), s32[]{:S(2)}) async-start(), calls=%async_computation.12 | async-start | bytes 4456448 | tf_op jit(solution)/shard_map/all_gather | solution.py:12
  980.9 84.9 %all-gather.69.cloned.1.call-start = ((), (), s32[]{:S(2)}) async-start(), calls=%async_computation.14 | async-start | bytes 4456448 | tf_op jit(solution)/shard_map/all_gather | solution.py:12
  981.5 126.7 %all-gather.67.cloned.1.call-start = ((), (), s32[]{:S(2)}) async-start(), calls=%async_computation.13 | async-start | bytes 4456448 | tf_op jit(solution)/shard_map/all_gather | solution.py:12
  982.1 176.7 %all-gather.71.cloned.1.call-start = ((), (), s32[]{:S(2)}) async-start(), calls=%async_computation.15 | async-start | bytes 4456448 | tf_op jit(solution)/shard_map/all_gather | solution.py:12
  1117.9 208.3 %all-gather.73.cloned.1.call-start = ((), (), s32[]{:S(2)}) async-start(), calls=%async_computation.16 | async-start | bytes 13369344 | tf_op jit(solution)/shard_map/all_gather | solution.py:12
  1164.2 65.8 %copy-start.5 = (f32[768,768]{0,1:T(8,128)S(1)}, f32[768,768]{0,1:T(8,128)}, u32[]{:S(2)}) copy-start(f32[768,768]{0,1:T(8,128)} %copy-done.4) | copy-start | bytes 7077892
  1232.9 157.7 %all-gather.79.cloned.1.call-start = ((), (), s32[]{:S(2)}) async-start(), calls=%async_computation.19 | async-start | bytes 4456448 | tf_op jit(solution)/shard_map/all_gather | solution.py:12
  1348.2 85.0 %all-gather.77.cloned.1.call-start = ((), (), s32[]{:S(2)}) async-start(), calls=%async_computation.18 | async-start | bytes 4456448 | tf_op jit(solution)/shard_map/all_gather | solution.py:12
  1348.9 126.7 %all-gather.75.cloned.1.call-start = ((), (), s32[]{:S(2)}) async-start(), calls=%async_computation.17 | async-start | bytes 4456448 | tf_op jit(solution)/shard_map/all_gather | solution.py:12
  (17 other events, 64.9 us)
Sparse Core Ops, SparseCore 0:
  9.5 46.3 all-gather.40
  130.3 93.1 all-gather.42
  245.5 42.2 all-gather.48
  289.6 40.6 all-gather.46
  332.0 40.6 all-gather.44
  382.6 40.6 all-gather.50
  498.3 93.1 all-gather.52
  613.6 42.2 all-gather.58
  657.8 40.6 all-gather.56
  700.2 40.6 all-gather.54
  750.0 40.6 all-gather.60
  865.8 93.1 all-gather.62
  981.0 42.2 all-gather.64
  1025.1 40.6 all-gather.68
  1067.5 40.6 all-gather.66
  1118.1 40.6 all-gather.70
  1233.0 93.1 all-gather.72
  1348.3 42.2 all-gather.78
  1392.5 40.6 all-gather.76
  1434.9 40.6 all-gather.74
